TPU v7x, 256 devices: a whole 4x4x8 slice. The times are simulated.
256 devices in a mesh: role: 4 (over x_lo, core), seq: 16 (over x_hi, z), tp: 4 (over y).
Axes of the slice: x: 4 (x_hi: 2, x_lo: 2; x = x_hi * 2 + x_lo), y: 4, z: 8, core: 2. Of those that a mesh axis runs over, the one named last changes fastest.
Arguments:
- gen_input: bfloat16 [2048, 64], P('seq'), may hold values from -6 to 6
- generated: bfloat16 [2048, 64], P('seq'), may hold values from -6 to 6
- noise: bfloat16 [2048, 64], P('seq'), may hold values from -6 to 6
- timesteps: int32 [7], replicated, may hold values from 20 to 979
- block_lengths: int32 [7], replicated, may hold values from 1 to 512, 2048 in all
- w_embed: bfloat16 [3, 5120, 64], P(None, 'seq'), may hold values from -0.75 to 0.75
- w_qkv: bfloat16 [3, 5120, 20, 3, 128], P(None, 'seq', 'tp')
- w_out: bfloat16 [3, 20, 128, 64], P(None, 'tp'), may hold values from -0.125 to 0.125
- modulation: float32 [4, 2, 5120], P('role'), may hold values from -3 to 3
Outputs:
- velocities: bfloat16 [4, 2048, 64], P('role', 'seq')
- qkv_grads: bfloat16 [4, 2048, 20, 3, 128], P('role', 'seq', 'tp')
Inputs may be any that keep to these rules, and one draw needn't show every extreme that they name: `block_lengths`: the block lengths sum to 2048; the longest is exactly 512.
All inputs are finite; a program needn't handle non-finite values. Where the computation divides by a largest or mean magnitude, that divisor is 1e-20 or more.
Results may differ from a plain program's by a relative error of at most 0.02.
Values may be sent and summed in bfloat16 or wider, within the bound.
A program may use at most 128 MiB of HBM per device.

v0:
```python
import jax
import jax.numpy as jnp
from jax import lax
from jax.sharding import PartitionSpec as P

eps_norm = 1e-06
masked_value = -1e30
guide_scale = 5.0


def block_index(positions, block_ends):
    return jnp.sum((positions[:, None] >= block_ends[None, :]).astype(jnp.int32), axis=1)


def noise_level(block_ids, timesteps):
    count = timesteps.shape[0]
    picks = (block_ids[:, None] == jnp.arange(count, dtype=jnp.int32)[None, :]).astype(jnp.float32)
    return jnp.sum(picks * timesteps.astype(jnp.float32)[None, :], axis=1) / 1000.0


def on_device(
    gen_input, generated, noise, timesteps, block_lengths, w_embed, w_qkv, w_out, modulation
):
    tok_rows = gen_input.shape[0]
    channels = gen_input.shape[1]
    seq_count = lax.axis_size("seq")
    all_rows = tok_rows * seq_count
    seq_rank = lax.axis_index("seq")
    role_index = lax.axis_index("role")
    net_index = jnp.where(role_index == 0, 0, jnp.where(role_index == 3, 2, 1))
    positions = seq_rank * tok_rows + jnp.arange(tok_rows, dtype=jnp.int32)
    every_token = jnp.arange(all_rows, dtype=jnp.int32)
    block_ends = jnp.cumsum(block_lengths)
    block_local = block_index(positions, block_ends)
    block_every = block_index(every_token, block_ends)
    sigma = noise_level(block_local, timesteps)[:, None]
    clean = generated.astype(jnp.float32)
    fresh = noise.astype(jnp.float32)
    noised = ((1.0 - sigma) * clean + sigma * fresh).astype(jnp.bfloat16)
    latents = jnp.where(role_index == 0, gen_input, noised)
    embed_part = lax.dynamic_index_in_dim(w_embed, net_index, 0, keepdims=False)
    qkv_part = lax.dynamic_index_in_dim(w_qkv, net_index, 0, keepdims=False)
    out_part = lax.dynamic_index_in_dim(w_out, net_index, 0, keepdims=False)
    modulate = modulation[0]
    head_local = qkv_part.shape[1]
    head_size = qkv_part.shape[3]
    column_count = head_local * 3 * head_size
    full_embed = lax.all_gather(embed_part, "seq", axis=0, tiled=True)
    embedded = jnp.dot(latents, full_embed.T, preferred_element_type=jnp.float32)
    mean_square = jnp.mean(embedded * embedded, axis=1, keepdims=True)
    normed = (
        embedded * lax.rsqrt(mean_square + eps_norm) * (1.0 + modulate[0]) + modulate[1]
    ).astype(jnp.bfloat16)
    piece = lax.all_gather(qkv_part, "seq", axis=0, tiled=True)
    projected = jnp.dot(
        normed, piece.reshape(piece.shape[0], column_count), preferred_element_type=jnp.float32
    )
    projected = projected.astype(jnp.bfloat16).reshape(tok_rows, head_local, 3, head_size)
    queries = projected[:, :, 0]
    keys_local = projected[:, :, 1]
    values_local = projected[:, :, 2]
    keys_every, values_every = (
        lax.all_gather(keys_local, "seq", axis=0, tiled=True),
        lax.all_gather(values_local, "seq", axis=0, tiled=True),
    )
    inv_root = head_size ** (-0.5)
    allowed = (block_every[None, :] <= block_local[:, None])[None]
    scores = (
        jnp.einsum("qhd,khd->hqk", queries, keys_every, preferred_element_type=jnp.float32)
        * inv_root
    )
    scores = jnp.where(allowed, scores, masked_value)
    top_score = jnp.max(scores, axis=2, keepdims=True)
    weights = jnp.exp(scores - top_score)
    totals = jnp.sum(weights, axis=2, keepdims=True)
    probs = weights / totals
    log_total = (top_score + jnp.log(totals))[:, :, 0]
    attended = jnp.einsum(
        "hqk,khd->qhd", probs.astype(jnp.bfloat16), values_every, preferred_element_type=jnp.float32
    ).astype(jnp.bfloat16)
    out_flat = out_part.reshape(head_local * head_size, channels)
    velocity_terms = jnp.dot(
        attended.reshape(tok_rows, head_local * head_size),
        out_flat,
        preferred_element_type=jnp.float32,
    )
    velocity = lax.psum(velocity_terms.astype(jnp.bfloat16), "tp")
    every_role = lax.all_gather(velocity[None], "role", axis=0, tiled=True)
    with_prompt = every_role[1].astype(jnp.float32)
    without_prompt = every_role[2].astype(jnp.float32)
    fake_velocity = every_role[3].astype(jnp.float32)
    real_velocity = without_prompt + guide_scale * (with_prompt - without_prompt)
    noised_wide = noised.astype(jnp.float32)
    real_clean = noised_wide - sigma * real_velocity
    fake_clean = noised_wide - sigma * fake_velocity
    distance = lax.psum(jnp.sum(jnp.abs(clean - real_clean)), "seq")
    spread = distance / (all_rows * channels) + eps_norm
    dmd_cotangent = (fake_clean - real_clean) / spread
    critic_cotangent = fake_velocity - (fresh - clean)
    cotangent = jnp.where(
        role_index == 0, dmd_cotangent, jnp.where(role_index == 3, critic_cotangent, 0.0)
    ).astype(jnp.bfloat16)
    grad_attended = jnp.dot(cotangent, out_flat.T, preferred_element_type=jnp.float32).astype(
        jnp.bfloat16
    )
    grad_attended = grad_attended.reshape(tok_rows, head_local, head_size)
    row_delta = jnp.einsum(
        "qhd,qhd->hq", grad_attended, attended, preferred_element_type=jnp.float32
    )
    grad_probs = jnp.einsum(
        "qhd,khd->hqk", grad_attended, values_every, preferred_element_type=jnp.float32
    )
    grad_scores = (probs * (grad_probs - row_delta[:, :, None]) * inv_root).astype(jnp.bfloat16)
    grad_query = jnp.einsum(
        "hqk,khd->qhd", grad_scores, keys_every, preferred_element_type=jnp.float32
    ).astype(jnp.bfloat16)
    query_every, grad_every = (
        lax.all_gather(queries, "seq", axis=0, tiled=True),
        lax.all_gather(grad_attended, "seq", axis=0, tiled=True),
    )
    total_every, delta_every = (
        lax.all_gather(log_total, "seq", axis=1, tiled=True),
        lax.all_gather(row_delta, "seq", axis=1, tiled=True),
    )
    allowed_keys = (block_local[None, :] <= block_every[:, None])[None]
    key_scores = (
        jnp.einsum("qhd,khd->hqk", query_every, keys_local, preferred_element_type=jnp.float32)
        * inv_root
    )
    key_scores = jnp.where(allowed_keys, key_scores, masked_value)
    key_probs = jnp.exp(key_scores - total_every[:, :, None])
    key_grad_probs = jnp.einsum(
        "qhd,khd->hqk", grad_every, values_local, preferred_element_type=jnp.float32
    )
    key_grad_scores = (key_probs * (key_grad_probs - delta_every[:, :, None]) * inv_root).astype(
        jnp.bfloat16
    )
    grad_key = jnp.einsum(
        "hqk,qhd->khd", key_grad_scores, query_every, preferred_element_type=jnp.float32
    ).astype(jnp.bfloat16)
    grad_value = jnp.einsum(
        "hqk,qhd->khd",
        key_probs.astype(jnp.bfloat16),
        grad_every,
        preferred_element_type=jnp.float32,
    ).astype(jnp.bfloat16)
    qkv_grads = jnp.stack([grad_query, grad_key, grad_value], axis=2)
    return (velocity[None], qkv_grads[None])


def solution(mesh):
    placed = (
        P("seq", None),
        P("seq", None),
        P("seq", None),
        P(),
        P(),
        P(None, "seq", None),
        P(None, "seq", "tp", None, None),
        P(None, "tp", None, None),
        P("role", None, None),
    )
    return jax.shard_map(
        on_device,
        mesh=mesh,
        in_specs=placed,
        out_specs=(P("role", "seq", None), P("role", "seq", "tp", None, None)),
        check_vma=False,
    )
```

profile of v0, /device:TPU:8, one launch (start us, length us, event | category | flops | bytes accessed | tf_op | source)
XLA Modules:
  0.0 699.3 jit_solution(4750260023737367680)
XLA Ops:
  7.3 2.4 constant_dynamic-slice_fusion.1
  9.7 0.8 constant_dynamic-slice_fusion.2
  10.6 0.2 copy.93
  10.7 78.4 %all-gather = bf16[1,5120,64]{2,0,1:T(2,128)(2,1)S(1)} all-gather(bf16[1,320,64]{2,0,1:T(2,128)(2,1)S(1)} %copy.93), channel_id=2, replica_groups=mesh['role'=4,'seq'=16,'tp'=4] {'seq'}, dimensions={1}, use_global_device_ids=true | all-gather | bytes 696320 | tf_op jit(solution)/shard_map/all_gather | solution.py:48
  89.1 1.5 copy.62
  90.6 0.7 convert_element_type.92
  91.2 0.8 reduce-window.8
  92.1 0.1 convert_reduce_fusion.1
  92.2 0.1 select_reduce_fusion
  92.3 0.3 copy-done.15
  92.6 0.2 copy-done.11
  92.7 1.3 multiply_reduce_fusion
  94.1 0.9 slice_add_fusion
  95.0 192.2 %all-gather.13.cloned.1.call-done = bf16[1,5120,5,3,128]{4,1,3,2,0:T(8,128)(2,1)} async-done(((bf16[1,320,5,3,128]{4,1,3,2,0:T(8,128)(2,1)}), bf16[1,5120,5,3,128]{4,1,3,2,0:T(8,128)(2,1)}) %all-gather.13.cloned.1.call-update) | async-done | bytes 19660816 | tf_op jit(solution)/shard_map/all_gather | solution.py:54
  287.2 24.0 %copy.63 = bf16[1,5120,5,3,128]{1,4,3,2,0:T(8,128)(2,1)} copy(bf16[1,5120,5,3,128]{4,1,3,2,0:T(8,128)(2,1)} %all-gather.13.cloned.1.call-done) | data formatting | bytes 39321600 | tf_op jit(solution)/shard_map/all_gather | solution.py:54
  311.2 10.4 %convolution_convert_fusion = bf16[128,1920]{1,0:T(8,128)(2,1)S(1)} fusion(bf16[5120,1920]{0,1:T(8,128)(2,1)} %bitcast.124, f32[128,5120]{1,0:T(8,128)S(1)} %get-tuple-element.20, f32[5120]{0:T(1024)S(1)} %bitcast.136, f32[5120]{0:T(1024)S(1)} %bitcast.135, f32[128]{0:T(128)S(1)} %add_rsqrt_fusion), kind=kOutput, calls=%fused_computation.28 | convolution fusion | flops 2519449600 | bytes 22815232 | tf_op jit(solution)/shard_map/dot_general | solution.py:55
  321.7 0.3 copy.64
  322.0 0.7 fusion.104
  322.7 0.8 copy.96
  323.6 0.7 all-gather.15.cloned.1.call-update
  324.3 0.8 copy.95
  325.3 0.1 convert_reduce_fusion
  325.4 0.2 broadcast_compare_fusion.1
  325.6 84.3 %all-gather.17.cloned.1.call-done = bf16[2048,5,1,128]{3,0,1,2:T(8,128)(2,1)} async-done(((bf16[128,5,1,128]{3,0,1,2:T(8,128)(2,1)}), bf16[2048,5,1,128]{3,0,1,2:T(8,128)(2,1)}) %all-gather.17.cloned.1.call-update) | async-done | bytes 2621456 | tf_op jit(solution)/shard_map/all_gather | solution.py:63
  409.9 3.0 fusion
  413.0 2.3 copy-done.2
  415.3 1.4 fusion.2
  416.6 83.1 %all-gather.15.cloned.1.call-done = bf16[2048,5,1,128]{0,3,1,2:T(8,128)(2,1)} async-done(((bf16[128,5,1,128]{0,3,1,2:T(8,128)(2,1)}), bf16[2048,5,1,128]{0,3,1,2:T(8,128)(2,1)}) %all-gather.15.cloned.1.call-update) | async-done | bytes 2621456 | tf_op jit(solution)/shard_map/all_gather | solution.py:64
  499.7 5.1 fusion.30
  504.8 0.2 fusion.54
  505.0 14.1 %psum.14 = bf16[1,128,64]{1,2,0:T(8,128)(2,1)S(1)} all-reduce(bf16[1,128,64]{1,2,0:T(8,128)(2,1)S(1)} %fusion.54), channel_id=1, replica_groups=mesh['role'=4,'seq'=16,'tp'=4] {'tp'}, use_global_device_ids=true, to_apply=%region_7.8 | all-reduce | flops 8192 | bytes 32768 | tf_op jit(solution)/shard_map/psum | solution.py:87
  519.1 5.2 all_gather.31
  524.3 1.3 fusion.79
  525.6 40.4 %psum.15 = f32[]{:T(128)} all-reduce(f32[]{:T(128)} %fusion.79), channel_id=1, replica_groups=mesh['role'=4,'seq'=16,'tp'=4] {'seq'}, use_global_device_ids=true, to_apply=%region_9.10 | all-reduce | flops 1 | bytes 8 | tf_op jit(solution)/shard_map/psum | solution.py:96
  566.6 1.5 convolution_convert_fusion.1
  568.1 1.1 copy.69
  569.2 0.8 copy.73
  570.1 1.7 broadcast_compare_fusion
  571.8 0.7 log_add_fusion
  572.4 38.3 %all_gather.33 = f32[5,2048]{1,0:T(8,128)} all-gather(f32[5,128]{1,0:T(8,128)S(1)} %log_add_fusion), channel_id=1, replica_groups=mesh['role'=4,'seq'=16,'tp'=4] {'seq'}, dimensions={1}, use_global_device_ids=true | all-gather | bytes 43520 | tf_op jit(solution)/shard_map/all_gather | solution.py:122
  610.8 40.6 %all_gather.35 = f32[5,2048]{1,0:T(8,128)} all-gather(f32[5,128]{1,0:T(8,128)S(1)} %fusion.59), channel_id=1, replica_groups=mesh['role'=4,'seq'=16,'tp'=4] {'seq'}, dimensions={1}, use_global_device_ids=true | all-gather | bytes 43520 | tf_op jit(solution)/shard_map/all_gather | solution.py:123
  651.4 4.9 fusion.8
  656.3 6.4 fusion.49
  662.7 14.4 %all-gather.11.cloned.1.call-done = bf16[2048,5,128]{2,0,1:T(8,128)(2,1)} async-done(((bf16[128,5,128]{2,0,1:T(8,128)(2,1)}), bf16[2048,5,128]{2,0,1:T(8,128)(2,1)}) %all-gather.11.cloned.1.call-update) | async-done | bytes 2621456 | tf_op jit(solution)/shard_map/all_gather | solution.py:119
  677.1 5.7 fusion.46
  682.8 7.8 %fusion.43 = bf16[128,5,1,128]{0,3,1,2:T(8,128)(2,1)} fusion(bf16[2048,5,1,128]{3,0,1,2:T(8,128)(2,1)S(1)} %copy-done.4, f32[5,2048,128]{2,1,0:T(8,128)} %fusion.8, bf16[2048,5,128]{2,0,1:T(8,128)(2,1)} %all-gather.11.cloned.1.call-done, f32[5,2048]{1,0:T(8,128)} %all_gather.35, f32[5,2048]{1,0:T(8,128)} %all_gather.33, ...), kind=kOutput, calls=%fused_computation.37 | convolution fusion | flops 680345600 | bytes 11157504 | tf_op jit(solution)/shard_map/hqk,qhd->khd/dot_general | solution.py:138
  690.7 1.0 maximum_bitcast_fusion
  691.7 1.0 copy.77
  (47 shorter events, 0.5 us)
Async XLA Ops:
  7.2 318.0 %copy-start = (bf16[3,5,128,64]{2,3,1,0:T(8,128)(2,1)S(1)}, bf16[3,5,128,64]{2,3,1,0:T(8,128)(2,1)}, u32[]{:S(2)}) copy-start(bf16[3,5,128,64]{2,3,1,0:T(8,128)(2,1)} %param.16) | copy-start | bytes 737284
  7.2 85.5 %copy-start.6 = (bf16[128,64]{0,1:T(8,128)(2,1)S(1)}, bf16[128,64]{0,1:T(8,128)(2,1)}, u32[]{:S(2)}) copy-start(bf16[128,64]{0,1:T(8,128)(2,1)} %param.11) | copy-start | bytes 49156
  7.2 85.5 %copy-start.7 = (bf16[128,64]{0,1:T(8,128)(2,1)S(1)}, bf16[128,64]{0,1:T(8,128)(2,1)}, u32[]{:S(2)}) copy-start(bf16[128,64]{0,1:T(8,128)(2,1)} %param.10) | copy-start | bytes 49156
  7.2 280.0 %all-gather.13.cloned.1.call-start = ((), (), s32[]{:S(2)}) async-start(), calls=%async_computation.1 | async-start | bytes 20889600 | tf_op jit(solution)/shard_map/all_gather | solution.py:54
  9.7 400.2 %all-gather.17.cloned.1.call-start = ((), (), s32[]{:S(2)}) async-start(), calls=%async_computation.3 | async-start | bytes 2785280 | tf_op jit(solution)/shard_map/all_gather | solution.py:63
  92.1 0.5 copy-start.15
  92.1 0.6 copy-start.11
  92.2 1.8 copy-start.13
  92.2 1.8 copy-start.14
  311.2 14.0 %copy-start.16 = (s32[7,1]{0,1:T(1,128)S(1)}, s32[7,1]{0,1:T(1,128)}, u32[]{:S(2)}) copy-start(s32[7,1]{0,1:T(1,128)} %copy-done.15) | copy-start | bytes 88
  311.2 14.1 %copy-start.12 = (s32[128]{0:T(128)S(1)}, s32[128]{0:T(128)}, u32[]{:S(2)}) copy-start(s32[128]{0:T(128)} %copy-done.11) | copy-start | bytes 1540
  323.5 176.2 %all-gather.15.cloned.1.call-start = ((), (), s32[]{:S(2)}) async-start(), calls=%async_computation.2 | async-start | bytes 2785280 | tf_op jit(solution)/shard_map/all_gather | solution.py:64
  324.2 327.2 %all-gather.19.cloned.1.call-start = ((), (), s32[]{:S(2)}) async-start(), calls=%async_computation.4 | async-start | bytes 2785280 | tf_op jit(solution)/shard_map/all_gather | solution.py:118
  325.1 352.0 %all-gather.11.cloned.1.call-start = ((), (), s32[]{:S(2)}) async-start(), calls=%async_computation | async-start | bytes 2785280 | tf_op jit(solution)/shard_map/all_gather | solution.py:119
  325.6 174.1 %copy-start.5 = (pred[128,2048]{1,0:T(8,128)(4,1)}, pred[128,2048]{1,0:T(8,128)(4,1)S(1)}, u32[]{:S(2)}) copy-start(pred[128,2048]{1,0:T(8,128)(4,1)S(1)} %broadcast_compare_fusion.1) | copy-start | bytes 786436
  412.9 2.3 copy-start.2
  416.6 88.2 %copy-start.9 = (f32[5,128]{1,0:T(8,128)}, f32[5,128]{1,0:T(8,128)S(1)}, u32[]{:S(2)}) copy-start(f32[5,128]{1,0:T(8,128)S(1)} %fusion.2) | copy-start | bytes 7684
  504.8 151.5 %copy-start.3 = (bf16[2048,5,1,128]{3,0,1,2:T(8,128)(2,1)S(1)}, bf16[2048,5,1,128]{3,0,1,2:T(8,128)(2,1)}, u32[]{:S(2)}) copy-start(bf16[2048,5,1,128]{3,0,1,2:T(8,128)(2,1)} %all-gather.17.cloned.1.call-done) | copy-start | bytes 7864324
  519.1 143.6 %copy-start.8 = (bf16[1,128,64]{1,2,0:T(8,128)(2,1)}, bf16[1,128,64]{1,2,0:T(8,128)(2,1)S(1)}, u32[]{:S(2)}) copy-start(bf16[1,128,64]{1,2,0:T(8,128)(2,1)S(1)} %psum.14) | copy-start | bytes 49156
  519.1 137.2 %copy-start.10 = (f32[5,128]{1,0:T(8,128)S(1)}, f32[5,128]{1,0:T(8,128)}, u32[]{:S(2)}) copy-start(f32[5,128]{1,0:T(8,128)} %copy-done.9) | copy-start | bytes 7684
  662.7 20.2 %copy-start.4 = (bf16[2048,5,1,128]{3,0,1,2:T(8,128)(2,1)S(1)}, bf16[2048,5,1,128]{3,0,1,2:T(8,128)(2,1)}, u32[]{:S(2)}) copy-start(bf16[2048,5,1,128]{3,0,1,2:T(8,128)(2,1)} %all-gather.19.cloned.1.call-done) | copy-start | bytes 7864324
  682.8 9.9 %copy-start.1 = (bf16[3,5,128,64]{2,3,1,0:T(8,128)(2,1)S(1)}, bf16[3,5,128,64]{2,3,1,0:T(8,128)(2,1)}, u32[]{:S(2)}) copy-start(bf16[3,5,128,64]{2,3,1,0:T(8,128)(2,1)} %param.16) | copy-start | bytes 737284
Sparse Core Ops, SparseCore 0:
  10.6 276.5 all-gather.12
  323.6 86.2 all-gather.16
  413.0 86.6 all-gather.14
  502.2 86.2 all-gather.18
  590.9 86.1 all-gather.10
where the time goes:
time: 700 us; the launch traced here: 699 us
  waiting for transfers between devices  375 us (54%)
  blocking collectives  217 us (31%)
  matrix products  46.4 us (7%)
  local copies, waits for them, and re-layouts  37.3 us (5%)
  between operations  14.7 us (2%)
  other arithmetic  8.99 us (1%)
    all_gather x1, waiting for transfers between devices, on_device(): piece = lax.all_gather(qkv_part, 'seq', axis=0, tiled=True)  192 us
    all_gather x1, waiting for transfers between devices, on_device(): lax.all_gather(keys_local, 'seq', axis=0, tiled=True)  84.3 us
    all_gather x1, waiting for transfers between devices, on_device(): lax.all_gather(values_local, 'seq', axis=0, tiled=True)  83.1 us
    all_gather x1, blocking collectives, on_device(): full_embed = lax.all_gather(embed_part, 'seq', axis=0, tiled=True)  78.4 us
    all_gather x1, blocking collectives, on_device(): lax.all_gather(row_delta, 'seq', axis=1, tiled=True)  40.6 us
    psum x1, blocking collectives, on_device(): distance = lax.psum(jnp.sum(jnp.abs(clean - real_clean)), 'seq')  40.4 us
    all_gather x1, blocking collectives, on_device(): lax.all_gather(log_total, 'seq', axis=1, tiled=True)  38.3 us
    all_gather x1, local copies, waits for them, and re-layouts, on_device(): piece = lax.all_gather(qkv_part, 'seq', axis=0, tiled=True)  24 us
  transfers between devices with their start and end apart: 5, of which 4 were waited for; matrix products, arithmetic and copies ran while one was open for 5% of the time, Pallas kernels for 0%

commit v1 on v0

v1 whole, which is shorter than its diff:
```python
import functools
import math

import jax
import jax.numpy as jnp
from jax import lax
from jax.experimental import pallas as pl
from jax.experimental.pallas import tpu as pltpu
from jax.sharding import PartitionSpec as P

MESH = pl.DeviceIdType.MESH
F32 = jnp.float32
BF16 = jnp.bfloat16

eps_norm = 1e-06
masked_value = -1e30
guide_scale = 5.0

ROWS = 160
ONE_A = 128
MARK = 129
ONE_B = 136
SIDE = 16


def nn(a, b):
    return lax.dot_general(a, b, (((1,), (0,)), ((), ())), preferred_element_type=F32)


def nt(a, b):
    return lax.dot_general(a, b, (((1,), (1,)), ((), ())), preferred_element_type=F32)


def iota(shape, dim):
    return lax.broadcasted_iota(jnp.int32, shape, dim)


def kernel(
    seq_count, tp_count, x_hi,
    gen_hbm, clean_hbm, fresh_hbm, steps_hbm, lens_hbm, emb_hbm, qkv_hbm, out_hbm, mod_hbm,
    vel, grads,
    gen, clean, fresh, steps, lens, mod, emb, wq, wo, lhs, part, rs, mall, ylocal, ybuf, slabs, mext,
    lq, lk, lv, lg, s_ref, p_ref, t1, u1, uk, uv, mx, vb, xb, zc, zl, cot_ref,
    load_sem, y_send, y_recv, w_send, w_recv, rs_send, rs_recv, ag_send, ag_recv,
    zc_send, zc_recv, zl_send, zl_recv, v_send, v_recv, x_send, x_recv,
):
    role = lax.axis_index("role")
    me = lax.axis_index("seq")
    tp = lax.axis_index("tp")
    channels, tok = gen.shape
    feats = emb.shape[1]
    heads, _, head = wo.shape
    blocks = lens.shape[0]
    every = seq_count * tok
    net = lax.div(role + 1, 2)
    per_chunk = s_ref.shape[2] // tok
    chunks = seq_count // per_chunk
    z_len = seq_count // x_hi
    my_x, my_z = lax.div(me, z_len), lax.rem(me, z_len)
    last = 3 * heads

    def at_offset(dx, dz):
        return lax.rem(my_x + dx, x_hi) * z_len + lax.rem(my_z + dz, z_len)

    def far_first(k):
        dx = 1 - lax.rem(k, 2)
        half = lax.div(k, 2)
        dz = z_len // 2 + (1 - 2 * lax.rem(half, 2)) * lax.div(half + 1, 2)
        return at_offset(dx, dz)

    def early_first(k):
        kind = lax.rem(my_z + lax.div(k, seq_count // 2), 2)
        j = lax.rem(k, seq_count // 2)
        dx = 1 - lax.rem(j, 2)
        half = lax.div(j, 2)
        even = z_len // 2 + 2 * (1 - 2 * lax.rem(half, 2)) * lax.div(half + 1, 2)
        odd = z_len // 2 - (1 - 2 * lax.rem(half, 2)) * (2 * lax.div(half, 2) + 1)
        return at_offset(dx, (1 - kind) * even + kind * odd)

    def block_at(who):
        x, z = lax.div(who, z_len), lax.rem(who, z_len)
        place = x * (z_len // 2) + lax.div(z, 2)
        first = place + lax.div(place, seq_count // 2 - 1) * (last - (seq_count // 2 - 1))
        late = lax.rem(z, 2)
        return (1 - late) * first + late * (place + seq_count // 2 - 1)

    def owner_of(b):
        half = seq_count // 2
        place, late = (half - 1, 0) if b == last else ((b, 0) if b < half - 1 else (b - half + 1, 1))
        return place // (z_len // 2) * z_len + 2 * (place % (z_len // 2)) + late

    my_block = block_at(me)

    barrier = pltpu.get_barrier_semaphore()

    def greet_seq(k, carry):
        pl.semaphore_signal(barrier, inc=1, device_id={"seq": far_first(k)}, device_id_type=MESH)
        return carry

    lax.fori_loop(0, seq_count - 1, greet_seq, 0)
    for d in range(1, tp_count):
        pl.semaphore_signal(barrier, inc=1, device_id={"tp": lax.rem(tp + d, tp_count)}, device_id_type=MESH)

    @pl.when(role == 0)
    def _():
        for other in range(1, 4):
            for t in range(tp_count):
                pl.semaphore_signal(barrier, inc=1, device_id={"role": other, "tp": t}, device_id_type=MESH)

    feat_start = pl.multiple_of(lax.div(me * feats, 128) * 128, 128)
    sources = (
        (emb_hbm.at[net], emb), (mod_hbm.at[:, pl.ds(feat_start, mod.shape[1])], mod), (steps_hbm, steps), (lens_hbm, lens),
        (gen_hbm, gen), (clean_hbm, clean), (fresh_hbm, fresh), (qkv_hbm.at[net], wq), (out_hbm.at[net], wo),
    )
    loads = [pltpu.make_async_copy(src, dst, load_sem.at[i]) for i, (src, dst) in enumerate(sources)]
    for load in loads:
        load.start()
    for load in loads[2:7]:
        load.wait()

    ends = []
    total = jnp.int32(0)
    for j in range(blocks):
        total = total + lens[j]
        ends.append(total)

    def block_of(positions):
        ids = jnp.zeros_like(positions)
        for j in range(blocks):
            ids = ids + (positions >= ends[j]).astype(jnp.int32)
        return ids

    lane_block = block_of(me * tok + iota((1, tok), 1))
    sigma = jnp.zeros((1, tok), F32)
    for j in range(blocks):
        sigma = sigma + jnp.where(lane_block == j, steps[j].astype(F32), 0.0)
    sigma = sigma / 1000.0
    clean32 = clean[...].astype(F32)
    fresh32 = fresh[...].astype(F32)
    noised = ((1.0 - sigma) * clean32 + sigma * fresh32).astype(BF16)
    latents = jnp.where(role == 0, gen[...].astype(F32), noised.astype(F32)).astype(BF16)
    quarter = channels // tp_count
    for t in range(tp_count):
        ylocal[t] = latents[t * quarter : (t + 1) * quarter]
    ybuf[tp, me] = ylocal[tp]

    @pl.when(role == 0)
    def _():
        pl.semaphore_wait(barrier, seq_count - 1 + tp_count - 1)

    @pl.when(role != 0)
    def _():
        pl.semaphore_wait(barrier, seq_count - 1 + tp_count - 1 + tp_count)

    def over_seq(src, dst, send, recv, order=far_first):
        def copy(who):
            return pltpu.make_async_remote_copy(
                src_ref=src(who), dst_ref=dst(me, who), send_sem=send.at[who], recv_sem=recv.at[me],
                device_id={"seq": who}, device_id_type=MESH,
            )

        def start():
            def body(k, carry):
                who = order(k)

                @pl.when(who != me)
                def _():
                    copy(who).start()

                return carry

            lax.fori_loop(0, seq_count, body, 0)

        def wait_sent():
            def body(k, carry):
                copy(far_first(k)).wait_send()
                return carry

            lax.fori_loop(0, seq_count - 1, body, 0)

        def wait_from(who):
            pltpu.make_async_remote_copy(
                src_ref=dst(who, me), dst_ref=dst(who, me), send_sem=send.at[who], recv_sem=recv.at[who],
                device_id={"seq": who}, device_id_type=MESH,
            ).wait_recv()

        def wait_all():
            def body(k, carry):
                wait_from(far_first(k))
                return carry

            lax.fori_loop(0, seq_count - 1, body, 0)

        return start, wait_sent, wait_from, wait_all

    y_start, y_wait_sent, _, y_wait_all = over_seq(
        lambda who: ybuf.at[tp, me], lambda who, at: ybuf.at[tp, who], y_send, y_recv
    )
    zc_start, zc_wait_sent, zc_wait_from, _ = over_seq(lambda who: zc.at[me], lambda who, at: zc.at[who], zc_send, zc_recv)
    zl_start, zl_wait_sent, zl_wait_from, _ = over_seq(lambda who: zl.at[me], lambda who, at: zl.at[who], zl_send, zl_recv)
    y_start()

    def rs_copy(who, rows):
        return pltpu.make_async_remote_copy(
            src_ref=part.at[block_at(who), 0:rows], dst_ref=rs.at[me, 0:rows], send_sem=rs_send.at[who],
            recv_sem=rs_recv.at[me], device_id={"seq": who}, device_id_type=MESH,
        )

    def rs_arrival(who, rows):
        return pltpu.make_async_remote_copy(
            src_ref=rs.at[who, 0:rows], dst_ref=rs.at[who, 0:rows], send_sem=rs_send.at[who],
            recv_sem=rs_recv.at[who], device_id={"seq": who}, device_id_type=MESH,
        )

    def ag_copy(who, rows):
        mine = mall.at[my_block, 0:rows]
        return pltpu.make_async_remote_copy(
            src_ref=mine, dst_ref=mine, send_sem=ag_send.at[who], recv_sem=ag_recv.at[me],
            device_id={"seq": who}, device_id_type=MESH,
        )

    long_rows, short_rows = channels + 16, channels

    def by_length(is_long, action):
        @pl.when(is_long)
        def _():
            action(long_rows)

        @pl.when(jnp.logical_not(is_long))
        def _():
            action(short_rows)

    def ag_wait(b):
        owner = owner_of(b)
        there = mall.at[b, 0 : long_rows if b == last else short_rows]

        @pl.when(me != owner)
        def _():
            pltpu.make_async_remote_copy(
                src_ref=there, dst_ref=there, send_sem=ag_send.at[owner], recv_sem=ag_recv.at[owner],
                device_id={"seq": owner}, device_id_type=MESH,
            ).wait_recv()

    loads[0].wait()
    loads[1].wait()
    odd = lax.rem(me, 2) == 1
    window = mod[...]
    mine = jnp.where(odd, window[:, 64 : 64 + feats], window[:, :feats])
    scale, shift = 1.0 + mine[0:1], mine[1:2]
    emb_now = emb[...]
    scaled = emb_now.astype(F32) * scale
    scaled_hi = scaled.astype(BF16)
    shift_rows = jnp.where(iota((16, feats), 0) == 0, shift, 0.0)
    shift_hi = shift_rows.astype(BF16)
    lhs[0:64, :] = scaled_hi
    lhs[64:80, :] = shift_hi
    lhs[80:144, :] = (scaled - scaled_hi.astype(F32)).astype(BF16)
    lhs[144:160, :] = (shift_rows - shift_hi.astype(F32)).astype(BF16)
    gram = nt(emb_now, jnp.concatenate([emb_now, emb_now], axis=0))
    gram_hi = gram.astype(BF16).astype(F32)
    left_half = iota((channels, 2 * channels), 1) < channels
    part[last, 0:64, :] = jnp.where(left_half, gram_hi, gram - gram_hi).astype(BF16)
    loads[7].wait()
    lhs_now = lhs[...]
    bias = jnp.zeros((16, head), F32)
    bias_row = iota((16, head), 0)
    for b in range(last):
        both = nn(lhs_now, wq[b // 3, b % 3])
        both = both[0:80] + both[80:160]
        part[b, 0:64, :] = both[0:64].astype(BF16)
        bias = jnp.where(bias_row == b, both[64:65], bias)
    part[last, 64:80, :] = bias.astype(BF16)
    rs[me] = part[my_block]

    def rs_step(k, carry):
        who = early_first(k)

        @pl.when(who != me)
        def _():
            by_length(block_at(who) == last, lambda rows: rs_copy(who, rows).start())

        return carry

    lax.fori_loop(0, seq_count, rs_step, 0)

    row_id = iota((16, every), 0)
    wide_block = block_of(iota((1, every), 1))
    extras = jnp.where(
        (row_id == 0) | (row_id == ONE_B - ONE_A) | ((row_id < ONE_B - ONE_A) & (wide_block == row_id - 1)), 1.0, 0.0
    ).astype(BF16)
    for s in range(seq_count):
        slabs[s, 128:144, :] = extras[:, s * tok : (s + 1) * tok]
        slabs[s, 144:160, :] = jnp.zeros((16, tok), BF16)

    y_wait_all()

    def quarter_copy(d):
        other = lax.rem(tp + d, tp_count)
        return pltpu.make_async_remote_copy(
            src_ref=ybuf.at[tp], dst_ref=ybuf.at[tp], send_sem=w_send.at[other], recv_sem=w_recv.at[tp],
            device_id={"tp": other}, device_id_type=MESH,
        )

    def quarter_arrival(d):
        other = lax.rem(tp + d, tp_count)
        return pltpu.make_async_remote_copy(
            src_ref=ybuf.at[other], dst_ref=ybuf.at[other], send_sem=w_send.at[other], recv_sem=w_recv.at[other],
            device_id={"tp": other}, device_id_type=MESH,
        )

    for d in (2, 1, 3):
        quarter_copy(d).start()

    def rs_wait(k, carry):
        who = far_first(k)
        by_length(my_block == last, lambda rows: rs_arrival(who, rows).wait_recv())
        return carry

    lax.fori_loop(0, seq_count - 1, rs_wait, 0)
    owned = jnp.zeros((64, 128), F32)
    for s in range(seq_count):
        owned = owned + rs[s, 0:64, :].astype(F32)
    folded = owned + pltpu.roll(owned, 64, 1)
    folded_hi = folded.astype(BF16).astype(F32)
    half = jnp.where(left_half, folded_hi, folded - folded_hi)
    mall[my_block, 0:64, :] = jnp.where(my_block == last, half, owned).astype(BF16)

    @pl.when(my_block == last)
    def _():
        owned_bias = jnp.zeros((16, 128), F32)
        for s in range(seq_count):
            owned_bias = owned_bias + rs[s, 64:80, :].astype(F32)
        mall[last, 64:80, :] = owned_bias.astype(BF16)

    def ag_step(k, carry):
        who = far_first(k)
        by_length(my_block == last, lambda rows: ag_copy(who, rows).start())
        return carry

    lax.fori_loop(0, seq_count - 1, ag_step, 0)

    for d in (2, 1, 3):
        quarter_arrival(d).wait_recv()
    ag_wait(last)
    y_all = jnp.concatenate(
        [jnp.concatenate([ybuf[t, s] for t in range(tp_count)], axis=0) for s in range(seq_count)], axis=1
    )
    y_wide = y_all.astype(F32)
    gram_y = nn(mall[last, 0:64, :], jnp.concatenate([y_all, y_all], axis=0))
    mean_square = jnp.sum(gram_y * y_wide, axis=0, keepdims=True) / (feats * seq_count)
    ry = y_wide * lax.rsqrt(jnp.maximum(mean_square, 0.0) + eps_norm)
    ry_hi = ry.astype(BF16)
    ry_lo = (ry - ry_hi.astype(F32)).astype(BF16)
    for s in range(seq_count):
        slabs[s, 0:64, :] = ry_hi[:, s * tok : (s + 1) * tok]
        slabs[s, 64:128, :] = ry_lo[:, s * tok : (s + 1) * tok]

    loads[8].wait()
    y_tok = jnp.transpose(slabs[me].astype(F32)).astype(BF16)
    tok_block = block_of(me * tok + iota((tok, ROWS), 0))
    lane = iota((tok, ROWS), 1)
    in_marks = (lane >= MARK) & (lane < MARK + blocks)
    later_keys = jnp.where(in_marks & (lane - MARK > tok_block), masked_value, 0.0)
    earlier_queries = jnp.where(in_marks & (lane - MARK < tok_block), masked_value, 0.0)
    root_scale = math.log2(math.e) / math.sqrt(head)
    inv_root = 1.0 / math.sqrt(head)
    first_row = iota((16, head), 0) == 0
    zlane = iota((tok, channels + SIDE), 1)
    side_lane = iota((tok, SIDE), 1)

    def split_const(rows, extra, const):
        low = const - const.astype(BF16).astype(F32)
        return jnp.where(lane == ONE_B, low, jnp.where(lane == ONE_A, const, rows + extra)).astype(BF16)

    def extend(b):
        mext[b, 0:64, :] = mall[b, 0:64, :]
        mext[b, 64:128, :] = mall[b, 0:64, :]
        mext[b, 128:144, :] = jnp.where(first_row, mall[last, 64:80, :].astype(F32)[b : b + 1], 0.0).astype(BF16)
        mext[b, 144:160, :] = jnp.zeros((16, head), BF16)

    def project(h):
        here = slice(h * tok, (h + 1) * tok)
        queries = nn(y_tok, mext[3 * h]).astype(BF16)
        q_rows = nt(queries, mext[3 * h + 1]) * root_scale
        lq[here, :] = split_const(q_rows, later_keys, q_rows[:, ONE_A : ONE_A + 1])

    def project_keys(h):
        here = slice(h * tok, (h + 1) * tok)
        keys = nn(y_tok, mext[3 * h + 1]).astype(BF16)
        values = nn(y_tok, mext[3 * h + 2]).astype(BF16)
        k_rows = nt(keys, mext[3 * h]) * root_scale
        minus_totals = jnp.where((side_lane == h) | (side_lane == heads + h), -1.0, 0.0).astype(BF16)
        lk[here, :] = jnp.concatenate(
            [split_const(k_rows, earlier_queries, k_rows[:, ONE_A : ONE_A + 1]), minus_totals], axis=1
        )
        v_rows = jnp.concatenate([nt(values, wo[h]), jnp.zeros((tok, SIDE), F32)], axis=1)
        lv[here, :] = jnp.where(zlane == channels + 2 * heads + h, -1.0, v_rows).astype(BF16)

    def chunk_of(buffer, c):
        return jnp.concatenate([buffer[c * per_chunk + i] for i in range(per_chunk)], axis=1)

    def attend(first, end):
        rows = slice(first * tok, end * tok)
        mx[rows, :] = jnp.full((rows.stop - rows.start, tok), masked_value, F32)

        def score_step(c, carry):
            scores = nn(lq[rows, :], chunk_of(slabs, c))
            s_ref[c, rows, :] = scores
            best = mx[rows, :]
            for i in range(per_chunk):
                best = jnp.maximum(best, scores[:, i * tok : (i + 1) * tok])
            mx[rows, :] = best
            return carry

        lax.fori_loop(0, chunks, score_step, 0)
        top = jnp.max(mx[rows, :], axis=1, keepdims=True)
        mx[rows, :] = jnp.broadcast_to(top, (rows.stop - rows.start, tok))
        t1[rows, :] = jnp.zeros((rows.stop - rows.start, ROWS), F32)

        def value_step(c, carry):
            best = mx[rows, :]
            weights = jnp.exp2(s_ref[c, rows, :] - jnp.concatenate([best] * per_chunk, axis=1)).astype(BF16)
            p_ref[c, rows, :] = weights
            t1[rows, :] += nt(weights, chunk_of(slabs, c))
            return carry

        lax.fori_loop(0, chunks, value_step, 0)
        totals = t1[rows, ONE_A : ONE_A + 1]
        t1[rows, :] = t1[rows, :] * (1.0 / totals)
        mx[rows, :] = jnp.where(iota((rows.stop - rows.start, tok), 1) == 0, mx[rows, :], totals)

    def velocity_terms(first, end):
        terms = jnp.zeros((channels, tok), F32)
        for h in range(first, end):
            attended = nn(t1[h * tok : (h + 1) * tok, :].astype(BF16), mext[3 * h + 2]).astype(BF16)
            terms = terms + nt(wo[h], attended)
        return terms

    split = 2
    for b in range(3 * split):
        ag_wait(b)
        extend(b)
    for h in range(split):
        project(h)
    attend(0, split)
    terms = velocity_terms(0, split)
    for b in range(3 * split, last):
        ag_wait(b)
        extend(b)
    for h in range(split, heads):
        project(h)
    attend(split, heads)
    terms = terms + velocity_terms(split, heads)

    vb[tp] = terms.astype(BF16)

    def term_copy(d):
        other = lax.rem(tp + d, tp_count)
        return pltpu.make_async_remote_copy(
            src_ref=vb.at[tp], dst_ref=vb.at[tp], send_sem=v_send.at[other], recv_sem=v_recv.at[tp],
            device_id={"tp": other}, device_id_type=MESH,
        )

    def term_arrival(d):
        other = lax.rem(tp + d, tp_count)
        return pltpu.make_async_remote_copy(
            src_ref=vb.at[other], dst_ref=vb.at[other], send_sem=v_send.at[other], recv_sem=v_recv.at[other],
            device_id={"tp": other}, device_id_type=MESH,
        )

    def role_copy(d):
        slot = (role - 1) * tp_count + tp
        other = lax.rem(tp + d, tp_count)
        return pltpu.make_async_remote_copy(
            src_ref=vb.at[tp], dst_ref=xb.at[slot], send_sem=x_send.at[other], recv_sem=x_recv.at[slot],
            device_id={"role": 0, "tp": other}, device_id_type=MESH,
        )

    @pl.when(role != 0)
    def _():
        for d in (2, 1, 3, 0):
            role_copy(d).start()

    for d in (2, 1, 3):
        term_copy(d).start()

    @pl.when((role == 0) | (role == 3))
    def _():
        for h in range(heads):
            project_keys(h)
        uk[...] = jnp.zeros(uk.shape, F32)
        uv[...] = jnp.zeros(uv.shape, F32)
        u1[...] = jnp.zeros(u1.shape, F32)

    for d in (1, 3, 2):
        term_arrival(d).wait_recv()
    velocity = vb[0].astype(F32)
    for t in range(1, tp_count):
        velocity = velocity + vb[t].astype(F32)
    velocity = velocity.astype(BF16)
    vel[...] = velocity

    def other_velocity(r):
        value = xb[(r - 1) * tp_count].astype(F32)
        for t in range(1, tp_count):
            value = value + xb[(r - 1) * tp_count + t].astype(F32)
        return value.astype(BF16).astype(F32)

    @pl.when(role == 0)
    def _():
        for i in range(3 * tp_count):
            pltpu.make_async_remote_copy(
                src_ref=xb.at[i], dst_ref=xb.at[i], send_sem=x_send.at[0], recv_sem=x_recv.at[i],
                device_id={"tp": lax.rem(tp + 1, tp_count)}, device_id_type=MESH,
            ).wait_recv()
        with_prompt, without_prompt = other_velocity(1), other_velocity(2)
        real = without_prompt + guide_scale * (with_prompt - without_prompt)
        real_clean = noised.astype(F32) - sigma * real
        fake_clean = noised.astype(F32) - sigma * other_velocity(3)
        cot_ref[0:64, :] = fake_clean - real_clean
        dist = jnp.sum(jnp.abs(clean32 - real_clean), keepdims=True)
        cot_ref[64:72, :] = jnp.broadcast_to(dist, (8, tok))

    @pl.when(role == 3)
    def _():
        cot_ref[0:64, :] = velocity.astype(F32) - (fresh32 - clean32)
        cot_ref[64:72, :] = jnp.zeros((8, tok), F32)

    def backward():
        cot = cot_ref[0:64, :]
        zc[me] = cot.astype(BF16)
        zc_start()
        cot_tok = jnp.transpose(cot).astype(BF16)
        side = iota((tok, tok), 1)
        columns = jnp.broadcast_to(cot_ref[64:65, 0:1], (tok, tok))
        for h in range(heads):
            here = slice(h * tok, (h + 1) * tok)
            grad_attended = nn(cot_tok, wo[h]).astype(BF16)
            g_rows = nt(grad_attended, mext[3 * h + 2])
            const = g_rows[:, ONE_A : ONE_A + 1]
            g_now = jnp.where(lane < ONE_A, g_rows, 0.0).astype(BF16)
            inner = jnp.sum(g_now.astype(F32) * t1[here, :], axis=1, keepdims=True)
            lg[here, :] = split_const(g_now.astype(F32), 0.0, -inner)
            log_total = mx[here, 0:1] + jnp.log2(mx[here, 1:2])
            log_high = log_total.astype(BF16).astype(F32)
            columns = jnp.where(side == h, log_high, columns)
            columns = jnp.where(side == heads + h, log_total - log_high, columns)
            columns = jnp.where(side == 2 * heads + h, inner + const, columns)
        zl[me] = jnp.transpose(columns)[0:SIDE].astype(BF16)
        zl_start()

        def query_step(c, carry):
            there = chunk_of(slabs, c)
            centred = nn(lg[...], there)
            grad_scores = (p_ref[c].astype(F32) * centred).astype(BF16)
            u1[...] += nt(grad_scores, there)
            return carry

        lax.fori_loop(0, chunks, query_step, 0)

        def key_step(c, carry):
            whos = [far_first(seq_count - 1 - per_chunk * c - i) for i in range(per_chunk)]

            @pl.when(c > 0)
            def _():
                zc_wait_from(whos[0])
                zl_wait_from(whos[0])

            for who in whos[1:]:
                zc_wait_from(who)
                zl_wait_from(who)
            there = jnp.concatenate([slabs[who] for who in whos], axis=1)
            cots = jnp.concatenate([zc[who] for who in whos], axis=1)
            sides = jnp.concatenate([zl[who] for who in whos], axis=1)
            probs = jnp.exp2(nn(lk[...], jnp.concatenate([there, sides], axis=0)))
            centred = nn(lv[...], jnp.concatenate([cots, sides], axis=0))
            uk[...] += nt((probs * centred).astype(BF16), there)
            uv[...] += nt(probs.astype(BF16), cots)
            return carry

        lax.fori_loop(0, chunks, key_step, 0)
        distance = jnp.zeros((1, tok), F32)
        for s in range(seq_count):
            distance = distance + zl[s].astype(F32)[SIDE - 1 : SIDE]
        spread = distance / (every * channels) + eps_norm
        factor = jnp.where(role == 0, 1.0 / spread, 1.0)
        for h in range(heads):
            here = slice(h * tok, (h + 1) * tok)
            rows_q = (u1[here, :] * (inv_root / mx[here, 1:2])).astype(BF16)
            grads[h, 0] = (nn(rows_q, mext[3 * h + 1]) * factor).astype(BF16)
            rows_k = (uk[here, :] * inv_root).astype(BF16)
            grads[h, 1] = (nn(rows_k, mext[3 * h]) * factor).astype(BF16)
            grads[h, 2] = (nn(uv[here, :].astype(BF16), wo[h]) * factor).astype(BF16)
        zc_wait_sent()
        zl_wait_sent()

    @pl.when((role == 0) | (role == 3))
    def _():
        backward()

    @pl.when((role != 0) & (role != 3))
    def _():
        grads[...] = jnp.zeros(grads.shape, BF16)

    y_wait_sent()

    def sent_step(k, carry):
        who = far_first(k)
        by_length(block_at(who) == last, lambda rows: rs_copy(who, rows).wait_send())
        by_length(my_block == last, lambda rows: ag_copy(who, rows).wait_send())
        return carry

    lax.fori_loop(0, seq_count - 1, sent_step, 0)
    for d in range(1, tp_count):
        quarter_copy(d).wait_send()
        term_copy(d).wait_send()

    @pl.when(role != 0)
    def _():
        for d in range(tp_count):
            role_copy(d).wait_send()


def solution(mesh):
    seq_count, tp_count = mesh.shape["seq"], mesh.shape["tp"]
    x_hi = 2

    def on_device(gen_input, generated, noise, timesteps, block_lengths, w_embed, w_qkv, w_out, modulation):
        tok, channels = gen_input.shape
        feats, heads, _, head = w_qkv.shape[1:]
        rows = heads * tok
        chunk = 2 * tok
        chunks = seq_count * tok // chunk
        vmem = pl.BlockSpec(memory_space=pltpu.VMEM)
        hbm = pl.BlockSpec(memory_space=pltpu.HBM)
        dma = pltpu.SemaphoreType.DMA
        velocity, grads = pl.pallas_call(
            functools.partial(kernel, seq_count, tp_count, x_hi),
            out_shape=(
                jax.ShapeDtypeStruct((channels, tok), BF16),
                jax.ShapeDtypeStruct((heads, 3, tok, head), BF16),
            ),
            in_specs=[hbm] * 9,
            out_specs=(vmem, vmem),
            scratch_shapes=[
                pltpu.VMEM((channels, tok), BF16),
                pltpu.VMEM((channels, tok), BF16),
                pltpu.VMEM((channels, tok), BF16),
                pltpu.SMEM(timesteps.shape, jnp.int32),
                pltpu.SMEM(block_lengths.shape, jnp.int32),
                pltpu.VMEM((2, feats + 64), F32),
                pltpu.VMEM((channels, feats), BF16),
                pltpu.VMEM((heads, 3, feats, head), BF16),
                pltpu.VMEM((heads, channels, head), BF16),
                pltpu.VMEM((160, feats), BF16),
                pltpu.VMEM((seq_count, 80, 128), BF16),
                pltpu.VMEM((seq_count, 80, 128), BF16),
                pltpu.VMEM((seq_count, 80, 128), BF16),
                pltpu.VMEM((tp_count, channels // tp_count, tok), BF16),
                pltpu.VMEM((tp_count, seq_count, channels // tp_count, tok), BF16),
                pltpu.VMEM((seq_count, ROWS, tok), BF16),
                pltpu.VMEM((3 * heads, ROWS, head), BF16),
                pltpu.VMEM((rows, ROWS), BF16),
                pltpu.VMEM((rows, ROWS + SIDE), BF16),
                pltpu.VMEM((rows, channels + SIDE), BF16),
                pltpu.VMEM((rows, ROWS), BF16),
                pltpu.VMEM((chunks, rows, chunk), F32),
                pltpu.VMEM((chunks, rows, chunk), BF16),
                pltpu.VMEM((rows, ROWS), F32),
                pltpu.VMEM((rows, ROWS), F32),
                pltpu.VMEM((rows, ROWS), F32),
                pltpu.VMEM((rows, channels), F32),
                pltpu.VMEM((rows, tok), F32),
                pltpu.VMEM((tp_count, channels, tok), BF16),
                pltpu.VMEM((3 * tp_count, channels, tok), BF16),
                pltpu.VMEM((seq_count, channels, tok), BF16),
                pltpu.VMEM((seq_count, SIDE, tok), BF16),
                pltpu.VMEM((channels + 8, tok), F32),
                dma((9,)),
                dma((seq_count,)), dma((seq_count,)),
                dma((tp_count,)), dma((tp_count,)),
                dma((seq_count,)), dma((seq_count,)),
                dma((seq_count,)), dma((seq_count,)),
                dma((seq_count,)), dma((seq_count,)),
                dma((seq_count,)), dma((seq_count,)),
                dma((tp_count,)), dma((tp_count,)),
                dma((tp_count,)), dma((3 * tp_count,)),
            ],
            compiler_params=pltpu.CompilerParams(
                collective_id=0, has_side_effects=True, vmem_limit_bytes=62 * 1024 * 1024
            ),
            name="distill",
        )(
            gen_input.T,
            generated.T,
            noise.T,
            timesteps,
            block_lengths,
            jnp.transpose(w_embed, (0, 2, 1)),
            jnp.transpose(w_qkv, (0, 2, 3, 1, 4)),
            jnp.transpose(w_out, (0, 1, 3, 2)),
            modulation[0],
        )
        return (velocity.T[None], jnp.transpose(grads, (2, 0, 1, 3))[None])

    placed = (
        P("seq", None),
        P("seq", None),
        P("seq", None),
        P(),
        P(),
        P(None, "seq", None),
        P(None, "seq", "tp", None, None),
        P(None, "tp", None, None),
        P("role", None, None),
    )
    return jax.shard_map(
        on_device,
        mesh=mesh,
        in_specs=placed,
        out_specs=(P("role", "seq", None), P("role", "seq", "tp", None, None)),
        check_vma=False,
    )
```

time: 700 us -> 59.6 us (0.09)
  waiting for transfers between devices: 375 us -> 0 us
  blocking collectives: 217 us -> 0 us
  Pallas kernels: 0 us -> 55.6 us
  matrix products: 46.4 us -> 0 us
  local copies, waits for them, and re-layouts: 37.3 us -> 3.18 us
  between operations: 14.7 us -> 0.64 us
  other arithmetic: 8.99 us -> 0 us
    all_gather x5 -> x0, waiting for transfers between devices: 374 us -> none  [the longest x1 192 us: on_device(): piece = lax.all_gather(qkv_part, 'seq', axis=0, tiled=True)]
    all_gather x4 -> x0, blocking collectives: 162 us -> none  [the longest x1 78.4 us: on_device(): full_embed = lax.all_gather(embed_part, 'seq', axis=0, tiled=True)]
    pallas_call x0 -> x1, Pallas kernels: none -> 55.6 us  [on_device(): pl.pallas_call(functools.partial(kernel, seq_count, tp_count, x_hi), out_...]
    psum x2 -> x0, blocking collectives: 54.4 us -> none  [the longest x1 40.4 us: on_device(): distance = lax.psum(jnp.sum(jnp.abs(clean - real_clean)), 'seq')]
    dot_general x10 -> x0, matrix products: 46.4 us -> none  [the longest x1 10.4 us: on_device(): jnp.dot(normed, piece.reshape(piece.shape[0], column_count), preferred_el...]
    all_gather x2 -> x0, local copies, waits for them, and re-layouts: 25.5 us -> none  [the longest x1 24 us: on_device(): piece = lax.all_gather(qkv_part, 'seq', axis=0, tiled=True)]
  transfers between devices with their start and end apart: 5 -> 0, of which waited for: 4 -> 0; matrix products, arithmetic and copies ran while one was open for 5% -> 0% of each run, Pallas kernels for 0% -> 0%
where the time goes in v1:
time: 59.6 us; the launch traced here: 59.4 us
  Pallas kernels  55.6 us (93%)
  local copies, waits for them, and re-layouts  3.18 us (5%)
  between operations  0.64 us (1%)
    pallas_call x1, Pallas kernels, on_device(): pl.pallas_call(functools.partial(kernel, seq_count, tp_count, x_hi), out_...  55.6 us
    unnamed x2, local copies, waits for them, and re-layouts  3.18 us

profile of v1, /device:TPU:8, one launch (start us, length us, event | category | flops | bytes accessed | tf_op | source)
XLA Modules:
  0.0 59.4 jit_solution(14203463428216473056)
XLA Ops:
  0.6 55.6 %distill.1 = (bf16[64,128]{1,0:T(8,128)(2,1)}, bf16[5,3,128,128]{3,2,1,0:T(8,128)(2,1)}) custom-call(bf16[64,128]{1,0:T(8,128)(2,1)} %bitcast.18, bf16[64,128]{1,0:T(8,128)(2,1)} %bitcast.19, bf16[64,128]{1,0:T(8,128)(2,1)} %bitcast.20, s32[7]{0:T(128)} %steps_hbm.1, s32[7]{0:T(128)} %lens_hbm.1, bf16[3,64,320]{2,1,0:T(8,128)(2,1)} %bitcast.16, ...), custom_call_target="tpu_custom_call" | custom-call | tf_op jit(solution)/shard_map/distill/pallas_call | solution.py:637
  56.2 1.3 %copy.13 = bf16[1,128,64]{1,2,0:T(8,128)(2,1)} copy(bf16[1,128,64]{1,2,0:T(8,128)(2,1)} %bitcast.21) | data formatting | bytes 32768
  57.6 1.9 %copy.14 = bf16[1,128,5,3,128]{4,1,3,2,0:T(8,128)(2,1)} copy(bf16[1,128,5,3,128]{4,1,3,2,0:T(8,128)(2,1)} %bitcast.14) | data formatting | bytes 983040

commit v2 on v1

v2 whole, which is shorter than its diff:
```python
import functools
import math

import jax
import jax.numpy as jnp
from jax import lax
from jax.experimental import pallas as pl
from jax.experimental.pallas import tpu as pltpu
from jax.sharding import PartitionSpec as P

MESH = pl.DeviceIdType.MESH
F32 = jnp.float32
BF16 = jnp.bfloat16

eps_norm = 1e-06
masked_value = -1e30
guide_scale = 5.0

ROWS = 144
MAIN = 80
ONE_A = 64
MARK = 65
ONE_B = 72
SIDE = 16


def nn(a, b):
    return lax.dot_general(a, b, (((1,), (0,)), ((), ())), preferred_element_type=F32)


def nt(a, b):
    return lax.dot_general(a, b, (((1,), (1,)), ((), ())), preferred_element_type=F32)


def iota(shape, dim):
    return lax.broadcasted_iota(jnp.int32, shape, dim)


def kernel(
    seq_count, tp_count, x_hi,
    gen_hbm, clean_hbm, fresh_hbm, steps_hbm, lens_hbm, emb_hbm, qkv_hbm, out_hbm, mod_hbm,
    vel, grads,
    gen, clean, fresh, steps, lens, mod, emb, wq, wo, lhs, part, rs, mall, ylocal, ybuf, slabs, mext,
    lq, lk, lv, lg, s_ref, p_ref, t1, u1, uk, uv, mx, vb, xb, zb, zl, pt_ref, gq, cot_ref, term_ref,
    load_sem, y_send, y_recv, w_send, w_recv, rs_send, rs_recv, ag_send, ag_recv,
    z_send, z_recv, zl_send, zl_recv, v_send, v_recv, x_send, x_recv,
):
    role = lax.axis_index("role")
    me = lax.axis_index("seq")
    tp = lax.axis_index("tp")
    channels, tok = gen.shape
    feats = emb.shape[1]
    heads, _, head = wo.shape
    blocks = lens.shape[0]
    every = seq_count * tok
    net = lax.div(role + 1, 2)
    per_chunk = s_ref.shape[2] // tok
    chunks = seq_count // per_chunk
    z_len = seq_count // x_hi
    my_x, my_z = lax.div(me, z_len), lax.rem(me, z_len)
    last = 3 * heads

    x_at = [lax.rem(my_x + dx, x_hi) * z_len for dx in range(x_hi)]
    z_at = [lax.rem(my_z + dz, z_len) for dz in range(z_len)]
    far_z = [4, 3, 5, 2, 6, 1, 7, 0]
    far_first = [x_at[dx] + z_at[dz] for dz in far_z for dx in (1, 0)][:-1]
    ring_first = [x_at[dx] + z_at[dz] for dx in (0, 1) for dz in far_z]
    self_in_ring = z_len - 1

    owner_order = [x * z_len + z for tier in ((0, 2, 4, 6), (1, 5), (3, 7)) for x in range(x_hi) for z in tier]
    last_owner = owner_order[0]
    block_owner = owner_order[1:] + [last_owner]

    def greeted_in_tiers():
        parity = lax.rem(my_z, 2)
        out = []
        for i in (2, 1, 3, 0):
            z = lax.rem(my_z + parity + 2 * i, z_len)
            out += [(x_at[1] + z, False), (x_at[0] + z, i == 0)]
        for residue in (1, 3):
            first = lax.rem(residue + z_len - my_z, 4)
            for step in (4, 0):
                z = lax.rem(my_z + first + step, z_len)
                out += [(x_at[1] + z, False), (x_at[0] + z, step == 0)]
        return out

    barrier = pltpu.get_barrier_semaphore()

    for who in far_first:
        pl.semaphore_signal(barrier, inc=1, device_id={"seq": who}, device_id_type=MESH)
    for d in range(1, tp_count):
        pl.semaphore_signal(barrier, inc=1, device_id={"tp": lax.rem(tp + d, tp_count)}, device_id_type=MESH)

    @pl.when(role == 0)
    def _():
        for other in range(1, 4):
            for t in range(tp_count):
                pl.semaphore_signal(barrier, inc=1, device_id={"role": other, "tp": t}, device_id_type=MESH)

    feat_start = pl.multiple_of(lax.div(me * feats, 128) * 128, 128)
    sources = (
        (emb_hbm.at[net], emb), (mod_hbm.at[:, pl.ds(feat_start, mod.shape[1])], mod), (steps_hbm, steps), (lens_hbm, lens),
        (gen_hbm, gen), (clean_hbm, clean), (fresh_hbm, fresh), (qkv_hbm.at[net], wq), (out_hbm.at[net], wo),
    )
    loads = [pltpu.make_async_copy(src, dst, load_sem.at[i]) for i, (src, dst) in enumerate(sources)]
    for load in loads:
        load.start()
    for load in loads[2:7]:
        load.wait()

    ends = []
    total = jnp.int32(0)
    for j in range(blocks):
        total = total + lens[j]
        ends.append(total)

    def block_of(positions):
        ids = jnp.zeros_like(positions)
        for j in range(blocks):
            ids = ids + (positions >= ends[j]).astype(jnp.int32)
        return ids

    lane_block = block_of(me * tok + iota((1, tok), 1))
    sigma = jnp.zeros((1, tok), F32)
    for j in range(blocks):
        sigma = sigma + jnp.where(lane_block == j, steps[j].astype(F32), 0.0)
    sigma = sigma / 1000.0
    clean32 = clean[...].astype(F32)
    fresh32 = fresh[...].astype(F32)
    noised = ((1.0 - sigma) * clean32 + sigma * fresh32).astype(BF16)
    latents = jnp.where(role == 0, gen[...].astype(F32), noised.astype(F32)).astype(BF16)
    quarter = channels // tp_count
    for t in range(tp_count):
        ylocal[t] = latents[t * quarter : (t + 1) * quarter]
    ybuf[tp, me] = ylocal[tp]

    loads[0].wait()
    loads[1].wait()
    odd = lax.rem(me, 2) == 1
    window = mod[...]
    mine = jnp.where(odd, window[:, 64 : 64 + feats], window[:, :feats])
    scale, shift = 1.0 + mine[0:1], mine[1:2]
    emb_now = emb[...]
    scaled = emb_now.astype(F32) * scale
    scaled_hi = scaled.astype(BF16)
    shift_rows = jnp.where(iota((16, feats), 0) == 0, shift, 0.0)
    shift_hi = shift_rows.astype(BF16)
    lhs[0:64, :] = scaled_hi
    lhs[64:80, :] = shift_hi
    lhs[80:144, :] = (scaled - scaled_hi.astype(F32)).astype(BF16)
    lhs[144:160, :] = (shift_rows - shift_hi.astype(F32)).astype(BF16)
    gram = nt(emb_now, jnp.concatenate([emb_now, emb_now], axis=0))
    gram_hi = gram.astype(BF16).astype(F32)
    left_half = iota((channels, 2 * channels), 1) < channels
    part[last_owner, 0:64, :] = jnp.where(left_half, gram_hi, gram - gram_hi).astype(BF16)
    loads[7].wait()
    lhs_now = lhs[...]
    bias = jnp.zeros((16, head), F32)
    bias_row = iota((16, head), 0)
    for b in range(last):
        both = nn(lhs_now, wq[b % heads, b // heads])
        both = both[0:80] + both[80:160]
        part[block_owner[b], 0:64, :] = both[0:64].astype(BF16)
        bias = jnp.where(bias_row == b, both[64:65], bias)
    part[last_owner, 64:80, :] = bias.astype(BF16)
    rs[me, 0:64, :] = part[me, 0:64, :]

    @pl.when(me == last_owner)
    def _():
        rs[last_owner, 64:80, :] = part[last_owner, 64:80, :]

    @pl.when(role == 0)
    def _():
        pl.semaphore_wait(barrier, seq_count - 1 + tp_count - 1)

    @pl.when(role != 0)
    def _():
        pl.semaphore_wait(barrier, seq_count - 1 + tp_count - 1 + tp_count)

    def over_seq(src, dst, send, recv, order):
        def copy(who):
            return pltpu.make_async_remote_copy(
                src_ref=src, dst_ref=dst(me), send_sem=send.at[who], recv_sem=recv.at[me],
                device_id={"seq": who}, device_id_type=MESH,
            )

        def start():
            for who in order:
                copy(who).start()

        def wait_sent():
            for who in order:
                copy(who).wait_send()

        def wait_from(whos):
            for who in whos:
                pltpu.make_async_remote_copy(
                    src_ref=dst(who), dst_ref=dst(who), send_sem=send.at[who], recv_sem=recv.at[who],
                    device_id={"seq": who}, device_id_type=MESH,
                ).wait_recv()

        return start, wait_sent, wait_from

    ring_others = ring_first[:self_in_ring] + ring_first[self_in_ring + 1 :]
    y_start, y_wait_sent, y_wait_from = over_seq(ybuf.at[tp, me], lambda who: ybuf.at[tp, who], y_send, y_recv, far_first)
    zl_start, zl_wait_sent, zl_wait_from = over_seq(zl.at[me], lambda who: zl.at[who], zl_send, zl_recv, far_first)
    z_start, z_wait_sent, z_wait_from = over_seq(zb.at[me], lambda who: zb.at[who], z_send, z_recv, far_first)

    def rs_copy(who, rows):
        return pltpu.make_async_remote_copy(
            src_ref=part.at[who, 0:rows], dst_ref=rs.at[me, 0:rows], send_sem=rs_send.at[who],
            recv_sem=rs_recv.at[me], device_id={"seq": who}, device_id_type=MESH,
        )

    def rs_arrival(who, rows):
        return pltpu.make_async_remote_copy(
            src_ref=rs.at[who, 0:rows], dst_ref=rs.at[who, 0:rows], send_sem=rs_send.at[who],
            recv_sem=rs_recv.at[who], device_id={"seq": who}, device_id_type=MESH,
        )

    def ag_copy(who, rows):
        mine = mall.at[me, 0:rows]
        return pltpu.make_async_remote_copy(
            src_ref=mine, dst_ref=mine, send_sem=ag_send.at[who], recv_sem=ag_recv.at[me],
            device_id={"seq": who}, device_id_type=MESH,
        )

    long_rows, short_rows = channels + 16, channels

    def by_length(is_long, action):
        @pl.when(is_long)
        def _():
            action(long_rows)

        @pl.when(jnp.logical_not(is_long))
        def _():
            action(short_rows)

    def ag_wait(b):
        owner = block_owner[b]
        there = mall.at[owner, 0 : long_rows if b == last else short_rows]

        @pl.when(me != owner)
        def _():
            pltpu.make_async_remote_copy(
                src_ref=there, dst_ref=there, send_sem=ag_send.at[owner], recv_sem=ag_recv.at[owner],
                device_id={"seq": owner}, device_id_type=MESH,
            ).wait_recv()

    for who, may_be_me in greeted_in_tiers():

        def send(who=who):
            by_length(who == last_owner, lambda rows: rs_copy(who, rows).start())

        if may_be_me:
            pl.when(who != me)(send)
        else:
            send()

    y_start()

    row_id = iota((16, every), 0)
    wide_block = block_of(iota((1, every), 1))
    extras = jnp.where(
        (row_id == 0) | (row_id == ONE_B - ONE_A) | ((row_id < ONE_B - ONE_A) & (wide_block == row_id - 1)), 1.0, 0.0
    ).astype(BF16)
    for s in range(seq_count):
        slabs[s, 64:80, :] = extras[:, s * tok : (s + 1) * tok]

    def rs_wait(rows):
        for who in far_first:
            rs_arrival(who, rows).wait_recv()

    by_length(me == last_owner, rs_wait)
    owned = jnp.zeros((64, 128), F32)
    for s in range(seq_count):
        owned = owned + rs[s, 0:64, :].astype(F32)
    folded = owned + pltpu.roll(owned, 64, 1)
    folded_hi = folded.astype(BF16).astype(F32)
    half = jnp.where(left_half, folded_hi, folded - folded_hi)
    mall[me, 0:64, :] = jnp.where(me == last_owner, half, owned).astype(BF16)

    @pl.when(me == last_owner)
    def _():
        owned_bias = jnp.zeros((16, 128), F32)
        for s in range(seq_count):
            owned_bias = owned_bias + rs[s, 64:80, :].astype(F32)
        mall[last_owner, 64:80, :] = owned_bias.astype(BF16)

    def ag_start(rows):
        for who in far_first:
            ag_copy(who, rows).start()

    by_length(me == last_owner, ag_start)

    y_wait_from(far_first)

    def quarter_copy(d):
        other = lax.rem(tp + d, tp_count)
        return pltpu.make_async_remote_copy(
            src_ref=ybuf.at[tp], dst_ref=ybuf.at[tp], send_sem=w_send.at[other], recv_sem=w_recv.at[tp],
            device_id={"tp": other}, device_id_type=MESH,
        )

    def quarter_arrival(d):
        other = lax.rem(tp + d, tp_count)
        return pltpu.make_async_remote_copy(
            src_ref=ybuf.at[other], dst_ref=ybuf.at[other], send_sem=w_send.at[other], recv_sem=w_recv.at[other],
            device_id={"tp": other}, device_id_type=MESH,
        )

    for d in (2, 1, 3):
        quarter_copy(d).start()

    for d in (2, 1, 3):
        quarter_arrival(d).wait_recv()
    ag_wait(last)
    y_all = jnp.concatenate(
        [jnp.concatenate([ybuf[t, s] for t in range(tp_count)], axis=0) for s in range(seq_count)], axis=1
    )
    y_wide = y_all.astype(F32)
    gram_y = nn(mall[last_owner, 0:64, :], jnp.concatenate([y_all, y_all], axis=0))
    mean_square = jnp.sum(gram_y * y_wide, axis=0, keepdims=True) / (feats * seq_count)
    ry = y_wide * lax.rsqrt(jnp.maximum(mean_square, 0.0) + eps_norm)
    ry_hi = ry.astype(BF16)
    ry_lo = (ry - ry_hi.astype(F32)).astype(BF16)
    for s in range(seq_count):
        slabs[s, 0:64, :] = ry_hi[:, s * tok : (s + 1) * tok]
        slabs[s, 80:144, :] = ry_lo[:, s * tok : (s + 1) * tok]

    loads[8].wait()
    y_tok = jnp.transpose(slabs[me].astype(F32)).astype(BF16)
    tok_block = block_of(me * tok + iota((tok, ROWS), 0))
    lane = iota((tok, ROWS), 1)
    in_marks = (lane >= MARK) & (lane < MARK + blocks)
    later_keys = jnp.where(in_marks & (lane - MARK > tok_block), masked_value, 0.0)
    earlier_queries = jnp.where(in_marks & (lane - MARK < tok_block), masked_value, 0.0)
    root_scale = math.log2(math.e) / math.sqrt(head)
    inv_root = 1.0 / math.sqrt(head)
    first_row = iota((16, head), 0) == 0
    zlane = iota((tok, channels + SIDE), 1)
    side_lane = iota((tok, SIDE), 1)

    def split_const(rows, extra, const):
        low = const - const.astype(BF16).astype(F32)
        at = iota(rows.shape, 1)
        return jnp.where(at == ONE_B, low, jnp.where(at == ONE_A, const, rows + extra)).astype(BF16)

    def extend(b):
        mext[b, 0:64, :] = mall[block_owner[b], 0:64, :]
        mext[b, 80:144, :] = mall[block_owner[b], 0:64, :]
        mext[b, 64:80, :] = jnp.where(first_row, mall[last_owner, 64:80, :].astype(F32)[b : b + 1], 0.0).astype(BF16)

    def project(h):
        here = slice(h * tok, (h + 1) * tok)
        queries = nn(y_tok, mext[h]).astype(BF16)
        q_rows = nt(queries, mext[heads + h]) * root_scale
        lq[here, :] = split_const(q_rows, later_keys, q_rows[:, ONE_A : ONE_A + 1])

    def project_keys(h):
        here = slice(h * tok, (h + 1) * tok)
        keys = nn(y_tok, mext[heads + h]).astype(BF16)
        values = nn(y_tok, mext[2 * heads + h]).astype(BF16)
        k_rows = nt(keys, mext[h]) * root_scale
        minus_totals = jnp.where((side_lane == h) | (side_lane == heads + h), -1.0, 0.0).astype(BF16)
        lk[here, :] = jnp.concatenate(
            [split_const(k_rows, earlier_queries, k_rows[:, ONE_A : ONE_A + 1]), minus_totals], axis=1
        )
        v_rows = jnp.concatenate([nt(values, wo[h]), jnp.zeros((tok, SIDE), F32)], axis=1)
        lv[here, :] = jnp.where(zlane == channels + h, -1.0, v_rows).astype(BF16)

    def chunk_of(buffer, c):
        return jnp.concatenate([buffer[c * per_chunk + i] for i in range(per_chunk)], axis=1)

    def attend(first, end):
        rows = slice(first * tok, end * tok)
        mx[rows, :] = jnp.full((rows.stop - rows.start, tok), masked_value, F32)

        def score_step(c):
            scores = nn(lq[rows, :], chunk_of(slabs, c))
            s_ref[c, rows, :] = scores
            best = mx[rows, :]
            for i in range(per_chunk):
                best = jnp.maximum(best, scores[:, i * tok : (i + 1) * tok])
            mx[rows, :] = best

        for c in range(chunks):
            score_step(c)
        top = jnp.max(mx[rows, :], axis=1, keepdims=True)
        mx[rows, :] = jnp.broadcast_to(top, (rows.stop - rows.start, tok))
        t1[rows, :] = jnp.zeros((rows.stop - rows.start, MAIN), F32)

        def value_step(c):
            best = mx[rows, :]
            weights = jnp.exp2(s_ref[c, rows, :] - jnp.concatenate([best] * per_chunk, axis=1)).astype(BF16)
            p_ref[c, rows, :] = weights
            t1[rows, :] += nt(weights, chunk_of(slabs, c)[0:MAIN])

        for c in range(chunks):
            value_step(c)
        totals = t1[rows, ONE_A : ONE_A + 1]
        t1[rows, :] = t1[rows, :] * (1.0 / totals)
        mx[rows, :] = jnp.where(iota((rows.stop - rows.start, tok), 1) == 0, mx[rows, :], totals)

    def velocity_terms(first, end):
        terms = jnp.zeros((channels, tok), F32)
        for h in range(first, end):
            attended = nn(t1[h * tok : (h + 1) * tok, :].astype(BF16), mext[2 * heads + h, 0:MAIN, :]).astype(BF16)
            term = nt(wo[h], attended)
            term_ref[h] = term
            terms = terms + term
        return terms

    for b in range(2 * heads):
        ag_wait(b)
        extend(b)
    for h in range(heads):
        project(h)
    attend(0, heads)
    for b in range(2 * heads, last):
        ag_wait(b)
        extend(b)
    terms = velocity_terms(0, heads)

    vb[tp] = terms.astype(BF16)

    def term_copy(d):
        other = lax.rem(tp + d, tp_count)
        return pltpu.make_async_remote_copy(
            src_ref=vb.at[tp], dst_ref=vb.at[tp], send_sem=v_send.at[other], recv_sem=v_recv.at[tp],
            device_id={"tp": other}, device_id_type=MESH,
        )

    def term_arrival(d):
        other = lax.rem(tp + d, tp_count)
        return pltpu.make_async_remote_copy(
            src_ref=vb.at[other], dst_ref=vb.at[other], send_sem=v_send.at[other], recv_sem=v_recv.at[other],
            device_id={"tp": other}, device_id_type=MESH,
        )

    def role_copy(d):
        slot = (role - 1) * tp_count + tp
        other = lax.rem(tp + d, tp_count)
        return pltpu.make_async_remote_copy(
            src_ref=vb.at[tp], dst_ref=xb.at[slot], send_sem=x_send.at[other], recv_sem=x_recv.at[slot],
            device_id={"role": 0, "tp": other}, device_id_type=MESH,
        )

    @pl.when(role != 0)
    def _():
        for d in (2, 1, 3, 0):
            role_copy(d).start()

        for d in (2, 1, 3):
            term_copy(d).start()

    @pl.when((role == 0) | (role == 3))
    def _():
        side = iota((tok, tok), 1)
        columns = jnp.zeros((tok, tok), F32)
        for h in range(heads):
            here = slice(h * tok, (h + 1) * tok)
            log_total = mx[here, 0:1] + jnp.log2(mx[here, 1:2])
            log_high = log_total.astype(BF16).astype(F32)
            columns = jnp.where(side == h, log_high, jnp.where(side == heads + h, log_total - log_high, columns))
        zl[me] = jnp.transpose(columns)[0:SIDE].astype(BF16)
        zl_start()
        for h in range(heads):
            project_keys(h)
        uk[...] = jnp.zeros(uk.shape, F32)
        uv[...] = jnp.zeros(uv.shape, F32)
        u1[...] = jnp.zeros(u1.shape, F32)

    y_wait_sent()

    for who in far_first:
        by_length(who == last_owner, lambda rows: rs_copy(who, rows).wait_send())

    def ag_sent(rows):
        for who in far_first:
            ag_copy(who, rows).wait_send()

    by_length(me == last_owner, ag_sent)
    for d in range(1, tp_count):
        quarter_copy(d).wait_send()

    def other_velocity(r):
        value = xb[(r - 1) * tp_count].astype(F32)
        for t in range(1, tp_count):
            value = value + xb[(r - 1) * tp_count + t].astype(F32)
        return value.astype(BF16).astype(F32)

    def own_velocity():
        for d in (1, 3, 2):
            term_arrival(d).wait_recv()
        value = vb[0].astype(F32)
        for t in range(1, tp_count):
            value = value + vb[t].astype(F32)
        vel[...] = value.astype(BF16)
        for d in range(1, tp_count):
            term_copy(d).wait_send()

    @pl.when(role != 0)
    def _():
        own_velocity()
        for d in range(tp_count):
            role_copy(d).wait_send()

    @pl.when(role == 0)
    def _():
        for i in range(3 * tp_count):
            pltpu.make_async_remote_copy(
                src_ref=xb.at[i], dst_ref=xb.at[i], send_sem=x_send.at[0], recv_sem=x_recv.at[i],
                device_id={"tp": lax.rem(tp + 1, tp_count)}, device_id_type=MESH,
            ).wait_recv()
        with_prompt, without_prompt = other_velocity(1), other_velocity(2)
        real = without_prompt + guide_scale * (with_prompt - without_prompt)
        real_clean = noised.astype(F32) - sigma * real
        fake_clean = noised.astype(F32) - sigma * other_velocity(3)
        cot_ref[0:64, :] = fake_clean - real_clean
        dist = jnp.sum(jnp.abs(clean32 - real_clean), keepdims=True)
        cot_ref[64:72, :] = jnp.broadcast_to(dist, (8, tok))

    @pl.when(role == 3)
    def _():
        cot_ref[0:64, :] = vel[...].astype(F32) - (fresh32 - clean32)
        cot_ref[64:72, :] = jnp.zeros((8, tok), F32)

    def backward():
        cot = cot_ref[0:64, :]
        cot16 = cot.astype(BF16)
        cot_wide = cot16.astype(F32)
        side_row = iota((SIDE, tok), 0)
        side_rows = jnp.broadcast_to(cot_ref[64:65, :], (SIDE, tok))
        for h in range(heads):
            delta = jnp.sum(cot_wide * term_ref[h], axis=0, keepdims=True)
            side_rows = jnp.where(side_row == h, delta, side_rows)
        zb[me, 0:64, :] = cot16
        zb[me, 64:80, :] = side_rows.astype(BF16)
        z_start()

        @pl.when(role == 0)
        def _():
            for d in (2, 1, 3):
                term_copy(d).start()

        cot_tok = jnp.transpose(cot).astype(BF16)
        for h in range(heads):
            here = slice(h * tok, (h + 1) * tok)
            grad_attended = nn(cot_tok, wo[h]).astype(BF16)
            g_rows = nt(grad_attended, mext[2 * heads + h, 0:MAIN, :])
            g_now = jnp.where(iota((tok, MAIN), 1) < ONE_A, g_rows, 0.0).astype(BF16).astype(F32)
            inner = jnp.sum(g_now * t1[here, :], axis=1, keepdims=True)
            lg[here, :] = split_const(g_now, 0.0, -inner)

        zl_wait_from(far_first)
        zl_wait_sent()

        @pl.when(role == 0)
        def _():
            own_velocity()


        def near_slabs(c):
            return ring_first[per_chunk * c : per_chunk * (c + 1)]

        def prob_step(c):
            whos = near_slabs(c)
            there = jnp.concatenate([slabs[who] for who in whos], axis=1)
            sides = jnp.concatenate([zl[who] for who in whos], axis=1)
            pt_ref[c] = jnp.exp2(nn(lk[...], jnp.concatenate([there, sides], axis=0))).astype(BF16)

        for c in range(chunks):
            prob_step(c)

        def query_step(c):
            there = chunk_of(slabs, c)[0:MAIN]
            centred = nn(lg[...], there)
            grad_scores = (p_ref[c].astype(F32) * centred).astype(BF16)
            u1[...] += nt(grad_scores, there)

        for c in range(chunks):
            query_step(c)
        for h in range(heads):
            here = slice(h * tok, (h + 1) * tok)
            rows_q = (u1[here, :] * (inv_root / mx[here, 1:2])).astype(BF16)
            gq[here, :] = nn(rows_q, mext[heads + h, 0:MAIN, :])

        def key_step(c):
            whos = near_slabs(c)

            there = jnp.concatenate([slabs[who, 0:MAIN, :] for who in whos], axis=1)
            cots = jnp.concatenate([zb[who] for who in whos], axis=1)
            probs = pt_ref[c]
            centred = nn(lv[...], cots)
            uk[...] += nt((probs.astype(F32) * centred).astype(BF16), there)
            uv[...] += nt(probs, cots[0:64])

        z_wait_from(ring_first[:self_in_ring])
        for c in range(chunks // 2):
            key_step(c)
        z_wait_sent()
        z_wait_from(ring_first[self_in_ring + 1 :])
        for c in range(chunks // 2, chunks):
            key_step(c)
        distance = jnp.zeros((1, tok), F32)
        for s in range(seq_count):
            distance = distance + zb[s, 64:80, :].astype(F32)[SIDE - 1 : SIDE]
        spread = distance / (every * channels) + eps_norm
        factor = jnp.where(role == 0, 1.0 / spread, 1.0)
        for h in range(heads):
            here = slice(h * tok, (h + 1) * tok)
            grads[h, 0] = (gq[here, :] * factor).astype(BF16)
            rows_k = (uk[here, :] * inv_root).astype(BF16)
            grads[h, 1] = (nn(rows_k, mext[h, 0:MAIN, :]) * factor).astype(BF16)
            grads[h, 2] = (nn(uv[here, :].astype(BF16), wo[h]) * factor).astype(BF16)


    @pl.when((role == 0) | (role == 3))
    def _():
        backward()

    @pl.when((role != 0) & (role != 3))
    def _():
        grads[...] = jnp.zeros(grads.shape, BF16)


def solution(mesh):
    seq_count, tp_count = mesh.shape["seq"], mesh.shape["tp"]
    x_hi = 2

    def on_device(gen_input, generated, noise, timesteps, block_lengths, w_embed, w_qkv, w_out, modulation):
        tok, channels = gen_input.shape
        feats, heads, _, head = w_qkv.shape[1:]
        rows = heads * tok
        chunk = 4 * tok
        chunks = seq_count * tok // chunk
        vmem = pl.BlockSpec(memory_space=pltpu.VMEM)
        hbm = pl.BlockSpec(memory_space=pltpu.HBM)
        dma = pltpu.SemaphoreType.DMA
        velocity, grads = pl.pallas_call(
            functools.partial(kernel, seq_count, tp_count, x_hi),
            out_shape=(
                pltpu.VMEM((channels, tok), BF16),
                pltpu.VMEM((heads, 3, tok, head), BF16),
            ),
            in_specs=[hbm] * 9,
            out_specs=(vmem, vmem),
            scratch_shapes=[
                pltpu.VMEM((channels, tok), BF16),
                pltpu.VMEM((channels, tok), BF16),
                pltpu.VMEM((channels, tok), BF16),
                pltpu.SMEM(timesteps.shape, jnp.int32),
                pltpu.SMEM(block_lengths.shape, jnp.int32),
                pltpu.VMEM((2, feats + 64), F32),
                pltpu.VMEM((channels, feats), BF16),
                pltpu.VMEM((heads, 3, feats, head), BF16),
                pltpu.VMEM((heads, channels, head), BF16),
                pltpu.VMEM((160, feats), BF16),
                pltpu.VMEM((seq_count, 80, 128), BF16),
                pltpu.VMEM((seq_count, 80, 128), BF16),
                pltpu.VMEM((seq_count, 80, 128), BF16),
                pltpu.VMEM((tp_count, channels // tp_count, tok), BF16),
                pltpu.VMEM((tp_count, seq_count, channels // tp_count, tok), BF16),
                pltpu.VMEM((seq_count, ROWS, tok), BF16),
                pltpu.VMEM((3 * heads, ROWS, head), BF16),
                pltpu.VMEM((rows, ROWS), BF16),
                pltpu.VMEM((rows, ROWS + SIDE), BF16),
                pltpu.VMEM((rows, channels + SIDE), BF16),
                pltpu.VMEM((rows, MAIN), BF16),
                pltpu.VMEM((chunks, rows, chunk), F32),
                pltpu.VMEM((chunks, rows, chunk), BF16),
                pltpu.VMEM((rows, MAIN), F32),
                pltpu.VMEM((rows, MAIN), F32),
                pltpu.VMEM((rows, MAIN), F32),
                pltpu.VMEM((rows, channels), F32),
                pltpu.VMEM((rows, tok), F32),
                pltpu.VMEM((tp_count, channels, tok), BF16),
                pltpu.VMEM((3 * tp_count, channels, tok), BF16),
                pltpu.VMEM((seq_count, channels + SIDE, tok), BF16),
                pltpu.VMEM((seq_count, SIDE, tok), BF16),
                pltpu.VMEM((chunks, rows, chunk), BF16),
                pltpu.VMEM((rows, head), F32),
                pltpu.VMEM((channels + 8, tok), F32),
                pltpu.VMEM((heads, channels, tok), F32),
                dma((9,)),
                dma((seq_count,)), dma((seq_count,)),
                dma((tp_count,)), dma((tp_count,)),
                dma((seq_count,)), dma((seq_count,)),
                dma((seq_count,)), dma((seq_count,)),
                dma((seq_count,)), dma((seq_count,)),
                dma((seq_count,)), dma((seq_count,)),
                dma((tp_count,)), dma((tp_count,)),
                dma((tp_count,)), dma((3 * tp_count,)),
            ],
            compiler_params=pltpu.CompilerParams(
                collective_id=0, has_side_effects=True, vmem_limit_bytes=56 * 1024 * 1024
            ),
            name="distill",
        )(
            gen_input.T,
            generated.T,
            noise.T,
            timesteps,
            block_lengths,
            jnp.transpose(w_embed, (0, 2, 1)),
            jnp.transpose(w_qkv, (0, 2, 3, 1, 4)),
            jnp.transpose(w_out, (0, 1, 3, 2)),
            modulation[0],
        )
        return (velocity.T[None], jnp.transpose(grads, (2, 0, 1, 3))[None])

    placed = (
        P("seq", None),
        P("seq", None),
        P("seq", None),
        P(),
        P(),
        P(None, "seq", None),
        P(None, "seq", "tp", None, None),
        P(None, "tp", None, None),
        P("role", None, None),
    )
    return jax.shard_map(
        on_device,
        mesh=mesh,
        in_specs=placed,
        out_specs=(P("role", "seq", None), P("role", "seq", "tp", None, None)),
        check_vma=False,
    )
```

time: 59.6 us -> 47.1 us (0.79)
  Pallas kernels: 55.6 us -> 44.9 us
  local copies, waits for them, and re-layouts: 3.18 us -> 1.39 us
    pallas_call x1, Pallas kernels: 55.6 us -> 44.9 us  [on_device(): pl.pallas_call(functools.partial(kernel, seq_count, tp_count, x_hi), out_...]
    unnamed x2, local copies, waits for them, and re-layouts: 3.18 us -> 1.39 us
where the time goes in v2:
time: 47.1 us; the launch traced here: 47 us
  Pallas kernels  44.9 us (95%)
  local copies, waits for them, and re-layouts  1.39 us (3%)
  between operations  0.64 us (1%)
    pallas_call x1, Pallas kernels, on_device(): pl.pallas_call(functools.partial(kernel, seq_count, tp_count, x_hi), out_...  44.9 us
    unnamed x2, local copies, waits for them, and re-layouts  1.39 us

profile of v2, /device:TPU:8, one launch (start us, length us, event | category | flops | bytes accessed | tf_op | source)
XLA Modules:
  0.0 47.0 jit_solution(4716374607452684501)
XLA Ops:
  0.6 44.9 %distill.1 = (bf16[64,128]{1,0:T(8,128)(2,1)S(1)}, bf16[5,3,128,128]{3,2,1,0:T(8,128)(2,1)S(1)}) custom-call(bf16[64,128]{1,0:T(8,128)(2,1)} %bitcast.19, bf16[64,128]{1,0:T(8,128)(2,1)} %bitcast.20, bf16[64,128]{1,0:T(8,128)(2,1)} %bitcast.21, s32[7]{0:T(128)} %steps_hbm.1, s32[7]{0:T(128)} %lens_hbm.1, bf16[3,64,320]{2,1,0:T(8,128)(2,1)} %bitcast.17, ...), custom_call_target="tpu_custom_call" | custom-call | tf_op jit(solution)/shard_map/distill/pallas_call | solution.py:641
  45.6 0.6 %copy.13 = bf16[1,128,64]{1,2,0:T(8,128)(2,1)} copy(bf16[1,128,64]{1,2,0:T(8,128)(2,1)S(1)} %bitcast.14) | data formatting | bytes 32768
  46.2 0.8 %copy.14 = bf16[1,128,5,3,128]{4,1,3,2,0:T(8,128)(2,1)} copy(bf16[1,128,5,3,128]{4,1,3,2,0:T(8,128)(2,1)S(1)} %bitcast.13) | data formatting | bytes 983040
